TPU v7x, 512 devices: a whole 4x4x16 slice. The times are simulated.
512 devices in a mesh: ex: 32 (over z, core), feat: 16 (over y, x).
Axes of the slice: x: 4, y: 4, z: 16, core: 2. Of those that a mesh axis runs over, the one named last changes fastest.
Arguments:
- features: bfloat16 [65536, 16384], P('ex', 'feat'), may hold values from -24 to 24
- test_matrix: bfloat16 [16384, 128], P('feat'), may hold values from -0.046875 to 0.046875
Outputs:
- first_range: float32 [65536, 128], P('ex')
- basis: float32 [65536, 128], P('ex')
- projected: float32 [128, 16384], P(None, 'feat')
All inputs are finite; a program needn't handle non-finite values.
Results may differ from a plain program's by a relative error of at most 0.0028.
Values sent between devices are 32-bit elements; how exact they have to be, the bound alone decides.
A program may use at most 64 MiB of HBM per device.

v0:
```python
import jax
import jax.numpy as jnp
from jax import lax
from jax.sharding import PartitionSpec as P

DIMS = 16384


def solve_rows(sketch, gram):
    lower = jnp.linalg.cholesky(gram)
    return jax.scipy.linalg.solve_triangular(lower, sketch.T, lower=True).T


def own_gram(sketch):
    return jnp.dot(
        sketch.T, sketch, preferred_element_type=jnp.float32, precision=lax.Precision.HIGHEST
    )


def first_pass(partial_value):
    sketch = lax.psum(partial_value, "feat")
    gram = lax.psum(own_gram(sketch), "ex")
    return solve_rows(sketch, gram)


def second_pass(partial_value):
    sketch = lax.psum(partial_value, "feat")
    gram = lax.psum(own_gram(sketch), "ex")
    return solve_rows(sketch, gram)


def shards(features, test_matrix):
    total_rows = features.shape[0] * lax.axis_size("ex")
    scale = jnp.sqrt(jnp.float32(total_rows))
    shrink = 1.0 / jnp.sqrt(jnp.float32(DIMS))
    partial_value = jnp.dot(features, test_matrix, preferred_element_type=jnp.float32)
    first_ortho = first_pass(partial_value)
    first_range = first_ortho * scale
    first_basis = first_ortho.astype(jnp.bfloat16)
    power_part = lax.dot_general(
        features, first_basis, (((0,), (0,)), ((), ())), preferred_element_type=jnp.float32
    )
    power_total = lax.psum(power_part, "ex")
    power = (power_total * shrink).astype(jnp.bfloat16)
    second_part = jnp.dot(features, power, preferred_element_type=jnp.float32)
    ortho = second_pass(second_part)
    basis = ortho * scale
    project_part = lax.dot_general(
        ortho.astype(jnp.bfloat16),
        features,
        (((0,), (0,)), ((), ())),
        preferred_element_type=jnp.float32,
    )
    projected = lax.psum(project_part, "ex")
    return (first_range, basis, projected)


def solution(mesh):
    return jax.shard_map(
        shards,
        mesh=mesh,
        in_specs=(P("ex", "feat"), P("feat", None)),
        out_specs=(P("ex", None), P("ex", None), P(None, "feat")),
        check_vma=False,
    )
```

profile of v0, /device:TPU:1, one launch (start us, length us, event | category | flops | bytes accessed | tf_op | source)
XLA Modules:
  0.0 1104.2 jit_solution(15901627047034573460)
XLA Ops:
  7.2 0.9 copy-done
  8.1 4.4 fusion.15
  12.6 121.7 %all-reduce.7.cloned.1.call-done = f32[2048,128]{1,0:T(8,128)} async-done(((f32[2048,128]{1,0:T(8,128)}), f32[2048,128]{1,0:T(8,128)}) %all-reduce.7.cloned.1.call-update) | async-done | bytes 1048592 | tf_op jit(solution)/shard_map/psum | solution.py:21
  134.3 4.0 fusion.16
  138.4 184.7 %all-reduce.9.cloned.1.call-done = f32[128,128]{0,1:T(8,128)} async-done(((f32[128,128]{0,1:T(8,128)}), f32[128,128]{0,1:T(8,128)}) %all-reduce.9.cloned.1.call-update) | async-done | bytes 65552 | tf_op jit(solution)/shard_map/psum | solution.py:22
  323.1 0.9 copy.6
  324.0 0.9 fusion.13
  324.9 11.7 %cholesky.44 = f32[128,128]{1,0:T(8,128)S(1)} custom-call(f32[128,128]{1,0:T(8,128)S(1)} %fusion.13), custom_call_target="Cholesky" | custom-call | tf_op jit(solution)/shard_map/jit(cholesky)/cholesky | solution.py:10
  336.6 0.6 compare_reduce_fusion.1
  337.3 0.7 fusion.8
  337.9 9.8 custom-call.6
  347.7 2.3 fusion.2
  350.0 3.7 convolution_bitcast_fusion.1
  353.8 0.2 all-reduce.13.cloned.1.call-start
  354.0 201.4 %all-reduce.11.cloned.1.call-done = f32[1024,128]{0,1:T(8,128)} async-done(((f32[1024,128]{0,1:T(8,128)}), f32[1024,128]{0,1:T(8,128)}) %all-reduce.11.cloned.1.call-update) | async-done | bytes 524304 | tf_op jit(solution)/shard_map/psum | solution.py:43
  555.3 4.8 convolution_bitcast_fusion
  560.3 116.1 %all-reduce.13.cloned.1.call-done = f32[2048,128]{0,1:T(8,128)} async-done(((f32[2048,128]{0,1:T(8,128)}), f32[2048,128]{0,1:T(8,128)}) %all-reduce.13.cloned.1.call-update) | async-done | bytes 1048592 | tf_op jit(solution)/shard_map/psum | solution.py:27
  676.4 3.3 fusion.17
  679.8 1.3 copy.9
  681.1 183.3 %all-reduce.15.cloned.1.call-done = f32[128,128]{0,1:T(8,128)} async-done(((f32[128,128]{0,1:T(8,128)}), f32[128,128]{0,1:T(8,128)}) %all-reduce.15.cloned.1.call-update) | async-done | bytes 65552 | tf_op jit(solution)/shard_map/psum | solution.py:28
  864.4 0.9 copy.8
  865.3 0.9 fusion.11
  866.2 11.7 %cholesky.55 = f32[128,128]{1,0:T(8,128)S(1)} custom-call(f32[128,128]{1,0:T(8,128)S(1)} %fusion.11), custom_call_target="Cholesky" | custom-call | tf_op jit(solution)/shard_map/jit(cholesky)/cholesky | solution.py:10
  877.9 0.6 compare_reduce_fusion
  878.6 0.7 fusion.9
  879.3 9.8 custom-call.7
  889.1 1.0 fusion
  890.1 3.7 fusion.4
  893.9 0.1 multiply_bitcast_fusion
  894.0 1.3 copy.10
  895.3 200.2 %all-reduce.17.cloned.1.call-done = f32[128,1024]{1,0:T(8,128)} async-done(((f32[128,1024]{1,0:T(8,128)}), f32[128,1024]{1,0:T(8,128)}) %all-reduce.17.cloned.1.call-update) | async-done | bytes 524304 | tf_op jit(solution)/shard_map/psum | solution.py:54
  1095.4 1.9 copy.19
  (17 shorter events, 0.5 us)
Async XLA Ops:
  7.2 1.0 copy-start
  7.2 127.1 %all-reduce.7.cloned.1.call-start = ((), (), s32[]{:S(2)}) async-start(), calls=%async_computation | async-start | bytes 2097152 | tf_op jit(solution)/shard_map/psum | solution.py:21
  12.6 310.5 %all-reduce.9.cloned.1.call-start = ((), (), s32[]{:S(2)}) async-start(), calls=%async_computation.1 | async-start | bytes 131072 | tf_op jit(solution)/shard_map/psum | solution.py:22
  138.3 417.0 %all-reduce.11.cloned.1.call-start = ((), (), s32[]{:S(2)}) async-start(), calls=%async_computation.2 | async-start | bytes 1048576 | tf_op jit(solution)/shard_map/psum | solution.py:43
  353.8 322.6 %all-reduce.13.cloned.1.call-start = ((), (), s32[]{:S(2)}) async-start(), calls=%async_computation.3 | async-start | bytes 2097152 | tf_op jit(solution)/shard_map/psum | solution.py:27
  560.2 304.2 %all-reduce.15.cloned.1.call-start = ((), (), s32[]{:S(2)}) async-start(), calls=%async_computation.4 | async-start | bytes 131072 | tf_op jit(solution)/shard_map/psum | solution.py:28
  676.4 212.7 %copy-start.1 = (f32[2048,128]{0,1:T(8,128)S(1)}, f32[2048,128]{0,1:T(8,128)}, u32[]{:S(2)}) copy-start(f32[2048,128]{0,1:T(8,128)} %all-reduce.13.cloned.1.call-done) | copy-start | bytes 3145732
  679.7 415.8 %all-reduce.17.cloned.1.call-start = ((), (), s32[]{:S(2)}) async-start(), calls=%async_computation.5 | async-start | bytes 1048576 | tf_op jit(solution)/shard_map/psum | solution.py:54
Sparse Core Ops, SparseCore 0:
  12.7 121.5 all-reduce.6
  138.4 184.5 all-reduce.8
  353.9 201.4 all-reduce.10
  560.3 115.9 all-reduce.12
  679.8 184.5 all-reduce.14
  894.0 201.4 all-reduce.16
where the time goes:
time: 1100 us
  waiting for transfers between devices  1010 us (92%)
  other arithmetic  47.6 us (4%)
  matrix products  27.2 us (2%)
  between operations  14.2 us (1%)
    psum x1, waiting for transfers between devices, shards(): power_total = lax.psum(power_part, 'ex')  201 us
    psum x1, waiting for transfers between devices, shards(): projected = lax.psum(project_part, 'ex')  200 us
    psum x1, waiting for transfers between devices, first_pass(): gram = lax.psum(own_gram(sketch), 'ex')  185 us
    psum x1, waiting for transfers between devices, second_pass(): gram = lax.psum(own_gram(sketch), 'ex')  183 us
    psum x1, waiting for transfers between devices, first_pass(): sketch = lax.psum(partial_value, 'feat')  122 us
    psum x1, waiting for transfers between devices, second_pass(): sketch = lax.psum(partial_value, 'feat')  116 us
    another operation x6, other arithmetic, solve_rows(): lower = jnp.linalg.cholesky(gram)  24.8 us
  transfers between devices with their start and end apart: 6, of which 6 were waited for; matrix products, arithmetic and copies ran while one was open for 0% of the time, Pallas kernels for 0%

commit v1 on v0

v1 whole, which is shorter than its diff:
```python
import functools

import jax
import jax.numpy as jnp
from jax import lax
from jax.experimental import pallas as pl
from jax.experimental.pallas import tpu as pltpu
from jax.sharding import PartitionSpec as P

DIMS = 16384
ROWS = 65536
RANK = 128
MESH = pl.DeviceIdType.MESH
F32 = jnp.float32
BF16 = jnp.bfloat16
HIGHEST = lax.Precision.HIGHEST
BLOCK = 8


def split3(value):
    high = value.astype(BF16)
    rest = value - high.astype(F32)
    middle = rest.astype(BF16)
    low = (rest - middle.astype(F32)).astype(BF16)
    return high, middle, low


def factor(work):
    lane = lax.broadcasted_iota(jnp.int32, (BLOCK, RANK), 1)

    def step(b, carry):
        at = pl.ds(pl.multiple_of(b * BLOCK, BLOCK), BLOCK)
        left = work[at, 0:RANK]
        right = work[at, RANK : 2 * RANK]
        diag = {}
        for j in range(BLOCK):
            column = jnp.sum(jnp.where(lane == b * BLOCK + j, left, 0.0), axis=1, keepdims=True)
            column = jnp.broadcast_to(column, (BLOCK, RANK))
            for i in range(j, BLOCK):
                diag[i, j] = column[i : i + 1, :]
        lrows = [left[i : i + 1, :] for i in range(BLOCK)]
        rrows = [right[i : i + 1, :] for i in range(BLOCK)]
        for j in range(BLOCK):
            inv = lax.rsqrt(diag[j, j])
            lrows[j] = lrows[j] * inv
            rrows[j] = rrows[j] * inv
            low = {i: diag[i, j] * inv for i in range(j + 1, BLOCK)}
            for i in range(j + 1, BLOCK):
                for k in range(j + 1, i + 1):
                    diag[i, k] = diag[i, k] - low[i] * low[k]
                lrows[i] = lrows[i] - low[i] * lrows[j]
                rrows[i] = rrows[i] - low[i] * rrows[j]
        left = jnp.concatenate(lrows, axis=0)
        right = jnp.concatenate(rrows, axis=0)
        below = jnp.where(lane >= (b + 1) * BLOCK, left, 0.0)
        both = jnp.concatenate([left, right], axis=1)
        work[...] -= lax.dot_general(
            below, both, (((0,), (0,)), ((), ())), preferred_element_type=F32, precision=HIGHEST
        )
        work[at, 0:RANK] = left
        work[at, RANK : 2 * RANK] = right
        return carry

    lax.fori_loop(0, RANK // BLOCK, step, 0)


class Grid:
    def __init__(self, nx, ny, nz):
        self.nx, self.ny, self.nz = nx, ny, nz
        ex, feat = lax.axis_index("ex"), lax.axis_index("feat")
        self.ex, self.feat = ex, feat
        self.x, self.y = lax.rem(feat, nx), lax.div(feat, nx)
        self.core, self.z = lax.rem(ex, 2), lax.div(ex, 2)

    def xpeer(self, k):
        to = lax.rem(self.x + k, self.nx)
        return to, (self.ex, self.y * self.nx + to)

    def ypeer(self, k):
        to = lax.rem(self.y + k, self.ny)
        return to, (self.ex, to * self.nx + self.x)

    def zpeer(self, k):
        to = lax.rem(self.z + k, self.nz)
        return to, (to * 2 + self.core, self.feat)

    def sibling(self):
        return (self.z * 2 + 1 - self.core, self.feat)

    def peers(self):
        out = [self.xpeer(k)[1] for k in range(1, self.nx)]
        out += [self.ypeer(k)[1] for k in range(1, self.ny)]
        return out + [self.sibling()]


def remote(src, dst, send, recv, to):
    return pltpu.make_async_remote_copy(
        src_ref=src, dst_ref=dst, send_sem=send, recv_sem=recv, device_id=to, device_id_type=MESH
    )


class FeatSum:
    SCRATCH = 12

    @staticmethod
    def scratch(nx, ny, rows):
        r, h = RANK // (nx * ny), rows // 2
        sems = [pltpu.SemaphoreType.DMA((4, nx - 1)), pltpu.SemaphoreType.DMA((4, nx - 1))]
        sems += [pltpu.SemaphoreType.DMA((4, ny - 1)), pltpu.SemaphoreType.DMA((4, ny - 1))]
        return [
            pltpu.VMEM((ny, nx, r, rows), F32),
            pltpu.VMEM((ny, nx, r, rows), F32),
            pltpu.VMEM((nx - 1, ny, r, h), F32),
            pltpu.VMEM((ny - 1, nx, r, h), F32),
            pltpu.VMEM((ny, r, h), F32),
            pltpu.VMEM((nx, r, h), F32),
            pltpu.VMEM((ny - 1, r, h), F32),
            pltpu.VMEM((nx - 1, r, h), F32),
        ] + sems

    def __init__(self, grid, refs):
        self.g = grid
        (self.part, self.full, self.r1a, self.r1b, self.s1a, self.s1b, self.r2a, self.r2b,
         self.xs, self.xr, self.ys, self.yr) = refs
        rows = self.part.shape[3]
        self.a, self.b = pl.ds(0, rows // 2), pl.ds(rows // 2, rows // 2)

    def over_x(self, n, src, dst):
        out = []
        for k in range(1, self.g.nx):
            to, device = self.g.xpeer(k)
            out.append(remote(src(to), dst(k - 1), self.xs.at[n, k - 1], self.xr.at[n, k - 1], device))
            out[-1].start()
        return out

    def over_y(self, n, src, dst):
        out = []
        for k in range(1, self.g.ny):
            to, device = self.g.ypeer(k)
            out.append(remote(src(to), dst(k - 1), self.ys.at[n, k - 1], self.yr.at[n, k - 1], device))
            out[-1].start()
        return out

    def start_a(self):
        self.c1a = self.over_x(0, lambda to: self.part.at[:, to, :, self.a], lambda k: self.r1a.at[k])

    def start_b(self):
        self.c1b = self.over_y(0, lambda to: self.part.at[to, :, :, self.b], lambda k: self.r1b.at[k])

    def finish(self):
        x, y = self.g.x, self.g.y
        full = self.full
        for c in self.c1a:
            c.wait_recv()
        self.s1a[...] = self.part[:, x, :, self.a] + sum(self.r1a[k] for k in range(self.g.nx - 1))
        c2a = self.over_y(1, lambda to: self.s1a.at[to], lambda k: self.r2a.at[k])
        for c in self.c1b:
            c.wait_recv()
        self.s1b[...] = self.part[y, :, :, self.b] + sum(self.r1b[k] for k in range(self.g.ny - 1))
        c2b = self.over_x(1, lambda to: self.s1b.at[to], lambda k: self.r2b.at[k])
        for c in c2a:
            c.wait_recv()
        full[y, x, :, self.a] = self.s1a[y] + sum(self.r2a[k] for k in range(self.g.ny - 1))
        own_a, own_b = full.at[y, x, :, self.a], full.at[y, x, :, self.b]
        c3a = self.over_y(2, lambda to: own_a, lambda k: own_a)
        for c in c2b:
            c.wait_recv()
        full[y, x, :, self.b] = self.s1b[x] + sum(self.r2b[k] for k in range(self.g.nx - 1))
        c3b = self.over_x(2, lambda to: own_b, lambda k: own_b)
        for c in c3a:
            c.wait_recv()
        col_a, row_b = full.at[:, x, :, self.a], full.at[y, :, :, self.b]
        c4a = self.over_x(3, lambda to: col_a, lambda k: col_a)
        for c in c3b:
            c.wait_recv()
        c4b = self.over_y(3, lambda to: row_b, lambda k: row_b)
        for c in c4a + c4b:
            c.wait_recv()
        self.sent = self.c1a + self.c1b + c2a + c2b + c3a + c3b + c4a + c4b

    def drain(self):
        for c in self.sent:
            c.wait_send()


class GramSum:
    SCRATCH = 9

    @staticmethod
    def scratch(nx, ny, nz):
        r = RANK // (nx * ny)
        return [
            pltpu.VMEM((r, RANK), F32),
            pltpu.VMEM((r, RANK), F32),
            pltpu.VMEM((r, RANK), F32),
            pltpu.VMEM((nz - 1, r, RANK), F32),
            pltpu.VMEM((ny, nx, r, RANK), F32),
            pltpu.SemaphoreType.DMA((1 + nx - 1 + ny - 1,)),
            pltpu.SemaphoreType.DMA((1 + nx - 1 + ny - 1,)),
            pltpu.SemaphoreType.DMA((nz - 1,)),
            pltpu.SemaphoreType.DMA((nz - 1,)),
        ]

    def __init__(self, grid, refs):
        self.g = grid
        (self.own, self.rc, self.pair, self.rz, self.full, self.ss, self.rs, self.zs, self.zr) = refs

    def start(self):
        self.c0 = remote(self.own, self.rc, self.ss.at[0], self.rs.at[0], self.g.sibling())
        self.c0.start()

    def zcopy(self, k):
        _, device = self.g.zpeer(k)
        return remote(self.pair, self.rz.at[k - 1], self.zs.at[k - 1], self.zr.at[k - 1], device)

    def over_z(self):
        self.c0.wait_recv()
        self.pair[...] = self.own[...] + self.rc[...]

        def go(k, carry):
            self.zcopy(k).start()
            return carry

        lax.fori_loop(1, self.g.nz, go, 0)

    def finish(self):
        g = self.g

        def wait(k, carry):
            self.zcopy(k).wait_recv()
            return carry

        lax.fori_loop(1, g.nz, wait, 0)
        self.full[g.y, g.x] = self.pair[...] + jnp.sum(self.rz[...], axis=0)
        own = self.full.at[g.y, g.x]
        cx = []
        for k in range(1, g.nx):
            cx.append(remote(own, own, self.ss.at[k], self.rs.at[k], g.xpeer(k)[1]))
            cx[-1].start()
        for c in cx:
            c.wait_recv()
        row = self.full.at[g.y]
        cy = []
        for k in range(1, g.ny):
            n = g.nx - 1 + k
            cy.append(remote(row, row, self.ss.at[n], self.rs.at[n], g.ypeer(k)[1]))
            cy[-1].start()
        for c in cy:
            c.wait_recv()
        self.sent = [self.c0] + cx + cy
        return self.full[...].reshape(RANK, RANK)

    def drain(self):
        for c in self.sent:
            c.wait_send()

        def wait(k, carry):
            self.zcopy(k).wait_send()
            return carry

        lax.fori_loop(1, self.g.nz, wait, 0)


class ExSum:
    SCRATCH = 10

    @staticmethod
    def scratch(nz, dims):
        r, h = RANK // nz, dims // 2
        return [
            pltpu.VMEM((2, nz, r, h), F32),
            pltpu.VMEM((nz, r, h), F32),
            pltpu.VMEM((nz, r, h), F32),
            pltpu.VMEM((nz - 1, r, h), F32),
            pltpu.VMEM((2, nz, r, h), F32),
            pltpu.SemaphoreType.DMA((2,)),
            pltpu.SemaphoreType.DMA((2,)),
            pltpu.SemaphoreType.DMA((2, nz - 1)),
            pltpu.SemaphoreType.DMA((2, nz - 1)),
        ]

    def __init__(self, grid, refs):
        self.g = grid
        (self.part, self.rc, self.pair, self.rz, self.full, self.cs, self.cr, self.zs, self.zr) = refs

    def start(self):
        other = 1 - self.g.core
        self.c0 = remote(self.part.at[other], self.rc, self.cs.at[0], self.cr.at[0], self.g.sibling())
        self.c0.start()

    def scatter(self, k):
        to, device = self.g.zpeer(k)
        return remote(self.pair.at[to], self.rz.at[k - 1], self.zs.at[0, k - 1], self.zr.at[0, k - 1], device)

    def gather(self, k):
        own = self.full.at[self.g.core, self.g.z]
        return remote(own, own, self.zs.at[1, k - 1], self.zr.at[1, k - 1], self.g.zpeer(k)[1])

    def loop(self, act):
        def body(k, carry):
            act(k)
            return carry

        lax.fori_loop(1, self.g.nz, body, 0)

    def over_z(self):
        self.c0.wait_recv()
        self.pair[...] = self.part[self.g.core] + self.rc[...]
        self.loop(lambda k: self.scatter(k).start())

    def spread(self):
        g = self.g
        self.loop(lambda k: self.scatter(k).wait_recv())
        self.full[g.core, g.z] = self.pair[g.z] + jnp.sum(self.rz[...], axis=0)
        self.loop(lambda k: self.gather(k).start())

    def arrive(self):
        self.loop(lambda k: self.gather(k).wait_recv())
        half = self.full.at[self.g.core]
        self.c1 = remote(half, half, self.cs.at[1], self.cr.at[1], self.g.sibling())
        self.c1.start()

    def drain(self):
        self.c0.wait_send()
        self.c1.wait_send()
        self.loop(lambda k: self.scatter(k).wait_send())
        self.loop(lambda k: self.gather(k).wait_send())


def kernel(nx, ny, nz, a_hbm, t_ref, first_hbm, basis_hbm, proj_hbm, a_ref, work, inv_ref, rows_ref, proj_ref,
           power_ref, a_sem, out_sem, *refs):
    g = Grid(nx, ny, nz)
    rows, dims = a_ref.shape
    refs = list(refs)

    def take(kind, n):
        out = kind(g, refs[:n])
        del refs[:n]
        return out

    sums = []
    for _ in range(2):
        sums.append((take(FeatSum, 12), take(GramSum, 9), take(ExSum, 9)))

    quarter = rows // 4
    loads = []
    for q in range(4):
        at = pl.ds(q * quarter, quarter)
        loads.append(pltpu.make_async_copy(a_hbm.at[at], a_ref.at[at], a_sem.at[q]))
        loads[-1].start()

    barrier = pltpu.get_barrier_semaphore()
    for device in g.peers():
        pl.semaphore_signal(barrier, inc=1, device_id=device, device_id_type=MESH)

    def greet(k, carry):
        pl.semaphore_signal(barrier, inc=1, device_id=g.zpeer(k)[1], device_id_type=MESH)
        return carry

    lax.fori_loop(1, nz, greet, 0)

    scale = jnp.sqrt(jnp.float32(ROWS))
    shrink = 1.0 / jnp.sqrt(jnp.float32(DIMS))
    shape = (ny, nx, RANK // (nx * ny), quarter)

    def round_trip(feat_sum, gram_sum, ex_sum):
        def rows_at(q):
            return feat_sum.full[:, :, :, q * quarter : (q + 1) * quarter].reshape(RANK, quarter)

        own = jnp.zeros((RANK // (nx * ny), RANK), F32)
        for q in range(4):
            mine = feat_sum.full[g.y, g.x, :, q * quarter : (q + 1) * quarter]
            own += lax.dot_general(mine, rows_at(q), (((1,), (1,)), ((), ())),
                                   preferred_element_type=F32, precision=HIGHEST)
        gram_sum.own[...] = own
        gram_sum.start()
        for q in range(4):
            terms = split3(rows_at(q))
            for n, term in enumerate(terms):
                rows_ref[n * RANK : (n + 1) * RANK, q * quarter : (q + 1) * quarter] = term
        h = dims // 2
        for s in range(2):
            half = 1 - g.core if s == 0 else g.core
            at = pl.ds(pl.multiple_of(half * h, h), h)
            prod = jnp.dot(rows_ref[...], a_ref[:, at], preferred_element_type=F32)
            prod = prod[:RANK] + prod[RANK : 2 * RANK] + prod[2 * RANK :]
            ex_sum.part[half] = prod.reshape(nz, RANK // nz, h)
            if s == 0:
                ex_sum.start()
                gram_sum.over_z()
        ex_sum.over_z()
        gram = gram_sum.finish()
        row = lax.broadcasted_iota(jnp.int32, (RANK, RANK), 0)
        column = lax.broadcasted_iota(jnp.int32, (RANK, RANK), 1)
        work[:, 0:RANK] = gram
        work[:, RANK : 2 * RANK] = jnp.where(row == column, 1.0, 0.0).astype(F32)
        ex_sum.spread()
        factor(work)
        inv_ref[...] = work[:, RANK : 2 * RANK]

    def write_rows(feat_sum, out_ref):
        def body(q, carry):
            at = pl.ds(pl.multiple_of(q * RANK, RANK), RANK)
            block = feat_sum.full[:, :, :, at].reshape(RANK, RANK)
            block = jnp.dot(inv_ref[...], block, preferred_element_type=F32, precision=HIGHEST)
            out_ref[at, :] = block.T * scale
            return carry

        lax.fori_loop(0, rows // RANK, body, 0)

    first, gram, ex = sums[0]
    first_out, basis_out = feat_rows_out = (refs[0], refs[1])
    test = t_ref[...].astype(F32).T.astype(BF16)
    for q in range(4):
        loads[q].wait()
        at = slice(q * quarter, (q + 1) * quarter)
        prod = lax.dot_general(test, a_ref[at, :], (((1,), (1,)), ((), ())), preferred_element_type=F32)
        first.part[:, :, :, at] = prod.reshape(shape)
        if q == 1:
            pl.semaphore_wait(barrier, nx - 1 + ny - 1 + nz - 1 + 1)
            first.start_a()
        if q == 3:
            first.start_b()
    first.finish()
    round_trip(first, gram, ex)
    write_rows(first, first_out)
    out1 = pltpu.make_async_copy(first_out, first_hbm, out_sem.at[0])
    out1.start()
    ex.arrive()

    second, gram2, ex2 = sums[1]
    h = dims // 2

    def power_half(half):
        w = ex.full[half].reshape(RANK, h)
        w = jnp.dot(inv_ref[...], w, preferred_element_type=F32, precision=HIGHEST)
        power_ref[half] = (w * shrink).astype(BF16)

    power_half(g.core)
    ex.c1.wait_recv()
    power_half(1 - g.core)
    for q in range(4):
        at = slice(q * quarter, (q + 1) * quarter)
        prod = lax.dot_general(power_ref[0], a_ref[at, 0:h], (((1,), (1,)), ((), ())), preferred_element_type=F32)
        prod += lax.dot_general(power_ref[1], a_ref[at, h:dims], (((1,), (1,)), ((), ())), preferred_element_type=F32)
        second.part[:, :, :, at] = prod.reshape(shape)
        if q == 1:
            second.start_a()
        if q == 3:
            second.start_b()
    second.finish()
    round_trip(second, gram2, ex2)
    write_rows(second, basis_out)
    out2 = pltpu.make_async_copy(basis_out, basis_hbm, out_sem.at[1])
    out2.start()
    ex2.arrive()

    def project_half(half):
        w = ex2.full[half].reshape(RANK, h)
        at = pl.ds(pl.multiple_of(half * h, h), h)
        proj_ref[:, at] = jnp.dot(inv_ref[...], w, preferred_element_type=F32, precision=HIGHEST)

    project_half(g.core)
    ex2.c1.wait_recv()
    project_half(1 - g.core)
    out3 = pltpu.make_async_copy(proj_ref, proj_hbm, out_sem.at[2])
    out3.start()
    for group in sums:
        for one in group:
            one.drain()
    out1.wait()
    out2.wait()
    out3.wait()


def shards(nx, ny, nz, features, test_matrix):
    rows, dims = features.shape
    hbm = pl.BlockSpec(memory_space=pl.ANY)
    scratch = [
        pltpu.VMEM((rows, dims), BF16),
        pltpu.VMEM((RANK, 2 * RANK), F32),
        pltpu.VMEM((RANK, RANK), F32),
        pltpu.VMEM((3 * RANK, rows), BF16),
        pltpu.VMEM((RANK, dims), F32),
        pltpu.VMEM((2, RANK, dims // 2), BF16),
        pltpu.SemaphoreType.DMA((4,)),
        pltpu.SemaphoreType.DMA((3,)),
    ]
    for _ in range(2):
        scratch += FeatSum.scratch(nx, ny, rows) + GramSum.scratch(nx, ny, nz) + ExSum.scratch(nz, dims)
    scratch += [pltpu.VMEM((rows, RANK), F32)] * 2
    return pl.pallas_call(
        functools.partial(kernel, nx, ny, nz),
        out_shape=(
            jax.ShapeDtypeStruct((rows, RANK), F32),
            jax.ShapeDtypeStruct((rows, RANK), F32),
            jax.ShapeDtypeStruct((RANK, dims), F32),
        ),
        in_specs=[hbm, pl.BlockSpec(memory_space=pltpu.VMEM)],
        out_specs=(hbm, hbm, hbm),
        scratch_shapes=scratch,
        compiler_params=pltpu.CompilerParams(
            collective_id=0, has_side_effects=True, vmem_limit_bytes=48 * 1024 * 1024
        ),
        cost_estimate=pl.CostEstimate(flops=6 * rows * dims * RANK * 2, bytes_accessed=8 << 20, transcendentals=256),
    )(features, test_matrix)


def solution(mesh):
    feat, ex = mesh.shape["feat"], mesh.shape["ex"]
    nx = {16: 4, 4: 2}[feat]
    return jax.shard_map(
        functools.partial(shards, nx, feat // nx, ex // 2),
        mesh=mesh,
        in_specs=(P("ex", "feat"), P("feat", None)),
        out_specs=(P("ex", None), P("ex", None), P(None, "feat")),
        check_vma=False,
    )
```

time: 1100 us -> 151 us (0.14)
  waiting for transfers between devices: 1010 us -> 0 us
  Pallas kernels: 0 us -> 147 us
  other arithmetic: 47.6 us -> 0 us
  matrix products: 27.2 us -> 0 us
  between operations: 14.2 us -> 0.65 us
    psum x6 -> x0, waiting for transfers between devices: 1010 us -> none  [the longest x1 201 us: shards(): power_total = lax.psum(power_part, 'ex')]
    pallas_call x0 -> x1, Pallas kernels: none -> 147 us  [shards(): pl.pallas_call(functools.partial(kernel, nx, ny, nz), out_shape=(jax.Shap...]
    another operation x10 -> x0, other arithmetic: 45.7 us -> none  [the longest x6 24.8 us: solve_rows(): lower = jnp.linalg.cholesky(gram)]
    dot_general x6 -> x0, matrix products: 23.9 us -> none  [the longest x2 7.25 us: own_gram(): jnp.dot(sketch.T, sketch, preferred_element_type=jnp.float32, precision=l...]
  transfers between devices with their start and end apart: 6 -> 0, of which waited for: 6 -> 0; matrix products, arithmetic and copies ran while one was open for 0% -> 0% of each run, Pallas kernels for 0% -> 0%
where the time goes in v1:
time: 151 us
  Pallas kernels  147 us (97%)
  local copies, waits for them, and re-layouts  3.68 us (2%)
    pallas_call x1, Pallas kernels, shards(): pl.pallas_call(functools.partial(kernel, nx, ny, nz), out_shape=(jax.Shap...  147 us
    unnamed x5, local copies, waits for them, and re-layouts  3.68 us

profile of v1, /device:TPU:1, one launch (start us, length us, event | category | flops | bytes accessed | tf_op | source)
XLA Modules:
  0.0 151.4 jit_solution(1219118734830243216)
XLA Ops:
  0.6 0.0 copy-start
  0.6 0.9 copy-done
  1.6 147.0 %shard_map.49 = (f32[2048,128]{1,0:T(8,128)S(1)}, f32[2048,128]{1,0:T(8,128)S(1)}, f32[128,1024]{1,0:T(8,128)S(1)}) custom-call(bf16[2048,1024]{1,0:T(8,128)(2,1)} %a_hbm.1, bf16[1024,128]{1,0:T(8,128)(2,1)S(1)} %copy-done), custom_call_target="tpu_custom_call" | custom-call | flops 3221225472 | bytes 8388608 | tf_op jit(solution)/shard_map/pallas_call | solution.py:492
  148.6 1.0 copy.8
  149.6 1.0 copy.9
  150.6 0.8 copy.10
Async XLA Ops:
  0.6 1.0 copy-start

commit v2 on v0

v2 whole, which is shorter than its diff:
```python
import functools

import jax
import jax.numpy as jnp
from jax import lax
from jax.experimental import pallas as pl
from jax.experimental.pallas import tpu as pltpu
from jax.sharding import PartitionSpec as P

DIMS = 16384
ROWS = 65536
RANK = 128
MESH = pl.DeviceIdType.MESH
F32 = jnp.float32
BF16 = jnp.bfloat16
HIGHEST = lax.Precision.HIGHEST
BLOCK = 8
CHUNKS = 2


def split(value):
    high = value.astype(BF16)
    return high, (value - high.astype(F32)).astype(BF16)


def factor(work, begin, end):
    lane = lax.broadcasted_iota(jnp.int32, (BLOCK, RANK), 1)

    def step(b, carry):
        at = pl.ds(pl.multiple_of(b * BLOCK, BLOCK), BLOCK)
        left = work[at, 0:RANK]
        right = work[at, RANK : 2 * RANK]
        diag = {}
        for j in range(BLOCK):
            column = jnp.sum(jnp.where(lane == b * BLOCK + j, left, 0.0), axis=1, keepdims=True)
            column = jnp.broadcast_to(column, (BLOCK, RANK))
            for i in range(j, BLOCK):
                diag[i, j] = column[i : i + 1, :]
        lrows = [left[i : i + 1, :] for i in range(BLOCK)]
        rrows = [right[i : i + 1, :] for i in range(BLOCK)]
        for j in range(BLOCK):
            inv = lax.rsqrt(diag[j, j])
            lrows[j] = lrows[j] * inv
            rrows[j] = rrows[j] * inv
            low = {i: diag[i, j] * inv for i in range(j + 1, BLOCK)}
            for i in range(j + 1, BLOCK):
                for k in range(j + 1, i + 1):
                    diag[i, k] = diag[i, k] - low[i] * low[k]
                lrows[i] = lrows[i] - low[i] * lrows[j]
                rrows[i] = rrows[i] - low[i] * rrows[j]
        left = jnp.concatenate(lrows, axis=0)
        right = jnp.concatenate(rrows, axis=0)
        below = jnp.where(lane >= (b + 1) * BLOCK, left, 0.0)
        both = jnp.concatenate([left, right], axis=1)
        work[...] -= lax.dot_general(
            below, both, (((0,), (0,)), ((), ())), preferred_element_type=F32, precision=HIGHEST
        )
        work[at, 0:RANK] = left
        work[at, RANK : 2 * RANK] = right
        return carry

    lax.fori_loop(begin, end, step, 0)


class Axis:
    def __init__(self, n, me, device):
        self.n, self.me, self.device = n, me, device

    def at(self, offset):
        return lax.rem(self.me + offset + self.n, self.n)

    def peer(self, offset):
        return self.device(self.at(offset))


class Grid:
    def __init__(self, nx, ny, nz):
        ex, feat = lax.axis_index("ex"), lax.axis_index("feat")
        x, y = lax.rem(feat, nx), lax.div(feat, nx)
        core, z = lax.rem(ex, 2), lax.div(ex, 2)
        self.core = core
        self.x = Axis(nx, x, lambda i: (ex, y * nx + i))
        self.y = Axis(ny, y, lambda i: (ex, i * nx + x))
        self.z = Axis(nz, z, lambda i: (i * 2 + core, feat))
        self.sibling = (z * 2 + 1 - core, feat)

    def greet(self):
        barrier = pltpu.get_barrier_semaphore()
        partners = [self.sibling]
        for axis in (self.x, self.y):
            partners += [axis.peer(k) for k in range(1, axis.n)]
        partners += [self.z.peer(k) for k in range(1, self.z.n)]
        for device in partners:
            pl.semaphore_signal(barrier, inc=1, device_id=device, device_id_type=MESH)
        return lambda: pl.semaphore_wait(barrier, len(partners))


class Copies:
    def __init__(self, send, recv):
        self.send_sem, self.recv_sem = send, recv
        self.started = []

    @staticmethod
    def scratch(n):
        return [pltpu.SemaphoreType.DMA((n,)), pltpu.SemaphoreType.DMA((n,))]

    def send(self, device, src, dst):
        n = len(self.started)
        copy = pltpu.make_async_remote_copy(
            src_ref=src, dst_ref=dst, send_sem=self.send_sem.at[n], recv_sem=self.recv_sem.at[n],
            device_id=device, device_id_type=MESH,
        )
        copy.start()
        self.started.append(copy)
        return copy

    def drain(self):
        for copy in self.started:
            copy.wait_send()


def far_first(axis, i):
    return lax.rem((2 * lax.rem(i, 2) - 1) * (axis.n // 2 - lax.div(i + 1, 2)) + axis.n, axis.n)


class Along:
    def __init__(self, axis, send, recv):
        self.axis, self.send_sem, self.recv_sem = axis, send, recv

    @staticmethod
    def scratch(n):
        return [pltpu.SemaphoreType.DMA((n - 1,)), pltpu.SemaphoreType.DMA((n - 1,))]

    def copy(self, i):
        to = self.axis.at(far_first(self.axis, i))
        return pltpu.make_async_remote_copy(
            src_ref=self.src(to), dst_ref=self.dst(i), send_sem=self.send_sem.at[i], recv_sem=self.recv_sem.at[i],
            device_id=self.axis.device(to), device_id_type=MESH,
        )

    def loop(self, act):
        def body(i, carry):
            act(self.copy(i))
            return carry

        if self.axis.n > 4:
            lax.fori_loop(0, self.axis.n - 1, body, 0)
        else:
            for i in range(self.axis.n - 1):
                body(i, 0)

    def start(self, src, dst):
        self.src, self.dst = src, dst
        self.loop(lambda copy: copy.start())

    def wait(self):
        self.loop(lambda copy: copy.wait_recv())

    def drain(self):
        self.loop(lambda copy: copy.wait_send())


class FeatSum:
    @staticmethod
    def scratch(nx, ny, ranks, rows):
        e, h = rows // (nx * ny), ranks // 2
        sems = []
        for _ in range(4):
            sems += Along.scratch(nx) + Along.scratch(ny)
        return [
            pltpu.VMEM((ny, nx, ranks, e), F32),
            pltpu.VMEM((ny, nx, ranks, e), F32),
            pltpu.VMEM((nx - 1, ny, h, e), F32),
            pltpu.VMEM((ny - 1, nx, h, e), F32),
            pltpu.VMEM((ny, h, e), F32),
            pltpu.VMEM((nx, h, e), F32),
            pltpu.VMEM((ny - 1, h, e), F32),
            pltpu.VMEM((nx - 1, h, e), F32),
        ] + sems

    def __init__(self, grid, refs):
        self.g = grid
        self.part, self.full, self.r1a, self.r1b, self.sa, self.sb, self.r2a, self.r2b = refs[:8]
        sems = refs[8:]
        self.ax = [Along(grid.x, *sems[4 * n : 4 * n + 2]) for n in range(4)]
        self.ay = [Along(grid.y, *sems[4 * n + 2 : 4 * n + 4]) for n in range(4)]

    def drain(self):
        for one in self.ax + self.ay:
            one.drain()

    def run(self):
        x, y = self.g.x, self.g.y
        part, full = self.part, self.full
        h = part.shape[2] // 2
        a, b = pl.ds(0, h), pl.ds(h, h)
        self.ax[0].start(lambda to: part.at[:, to, a], lambda i: self.r1a.at[i])
        self.ay[0].start(lambda to: part.at[to, :, b], lambda i: self.r1b.at[i])
        yield
        self.ax[0].wait()
        self.sa[...] = part[:, x.me, a] + sum(self.r1a[i] for i in range(x.n - 1))
        self.ay[1].start(lambda to: self.sa.at[to], lambda i: self.r2a.at[i])
        self.ay[0].wait()
        self.sb[...] = part[y.me, :, b] + sum(self.r1b[i] for i in range(y.n - 1))
        self.ax[1].start(lambda to: self.sb.at[to], lambda i: self.r2b.at[i])
        yield
        own_a, own_b = full.at[y.me, x.me, a], full.at[y.me, x.me, b]
        self.ay[1].wait()
        own_a[...] = self.sa[y.me] + sum(self.r2a[i] for i in range(y.n - 1))
        self.ay[2].start(lambda to: own_a, lambda i: own_a)
        self.ax[1].wait()
        own_b[...] = self.sb[x.me] + sum(self.r2b[i] for i in range(x.n - 1))
        self.ax[2].start(lambda to: own_b, lambda i: own_b)
        yield
        column_a, row_b = full.at[:, x.me, a], full.at[y.me, :, b]
        self.ay[2].wait()
        self.ax[3].start(lambda to: column_a, lambda i: column_a)
        self.ax[2].wait()
        self.ay[3].start(lambda to: row_b, lambda i: row_b)
        yield
        self.ax[3].wait()
        self.ay[3].wait()


class GramSum:
    @staticmethod
    def scratch(nx, ny, nz):
        r = RANK // (nx * ny)
        return [
            pltpu.VMEM((r, RANK), F32),
            pltpu.VMEM((r, RANK), F32),
            pltpu.VMEM((r, RANK), F32),
            pltpu.VMEM((nz - 1, r, RANK), F32),
            pltpu.VMEM((ny, nx, r, RANK), F32),
        ] + Copies.scratch(1) + Along.scratch(nz) + Along.scratch(nx) + Along.scratch(ny)

    def __init__(self, grid, refs):
        self.g = grid
        self.own, self.rc, self.pair, self.rz, self.full = refs[:5]
        self.copies = Copies(*refs[5:7])
        self.az, self.ax, self.ay = Along(grid.z, *refs[7:9]), Along(grid.x, *refs[9:11]), Along(grid.y, *refs[11:13])

    def drain(self):
        self.copies.drain()
        for one in (self.az, self.ax, self.ay):
            one.drain()

    def run(self):
        g = self.g
        across = self.copies.send(g.sibling, self.own, self.rc)
        yield
        across.wait_recv()
        self.pair[...] = self.own[...] + self.rc[...]
        self.az.start(lambda to: self.pair, lambda i: self.rz.at[i])
        yield
        self.az.wait()
        self.full[g.y.me, g.x.me] = self.pair[...] + jnp.sum(self.rz[...], axis=0)
        own, row = self.full.at[g.y.me, g.x.me], self.full.at[g.y.me]
        self.ax.start(lambda to: own, lambda i: own)
        yield
        self.ax.wait()
        self.ay.start(lambda to: row, lambda i: row)
        yield
        self.ay.wait()


class ExSum:
    @staticmethod
    def shape(nz, ranks, dims):
        r = max(8, ranks // nz)
        groups = ranks // r
        across = nz // groups
        return groups, across, r, dims // 2 // across

    @staticmethod
    def scratch(nz, ranks, dims):
        groups, across, r, w = ExSum.shape(nz, ranks, dims)
        blocks = (groups, across, r, w)
        return [
            pltpu.VMEM((2,) + blocks, F32),
            pltpu.VMEM(blocks, F32),
            pltpu.VMEM(blocks, F32),
            pltpu.VMEM((nz - 1, r, w), F32),
            pltpu.VMEM((2,) + blocks, F32),
        ] + Copies.scratch(2) + Along.scratch(nz) + Along.scratch(nz)

    def __init__(self, grid, refs):
        self.g = grid
        self.part, self.rc, self.pair, self.rz, self.full = refs[:5]
        self.copies = Copies(*refs[5:7])
        self.out, self.back = Along(grid.z, *refs[7:9]), Along(grid.z, *refs[9:11])

    def drain(self):
        self.copies.drain()
        self.out.drain()
        self.back.drain()

    def put(self, side, value):
        _, groups, across, r, w = self.part.shape
        for j in range(across):
            self.part[side, :, j] = value[:, j * w : (j + 1) * w].reshape(groups, r, w)

    def get(self, side):
        _, groups, across, r, w = self.part.shape
        return jnp.concatenate([self.full[side, :, j].reshape(groups * r, w) for j in range(across)], axis=1)

    def start(self):
        self.c0 = self.copies.send(self.g.sibling, self.part.at[1 - self.g.core], self.rc)

    def run(self):
        z, core = self.g.z, self.g.core
        across = self.part.shape[2]
        place = lambda i: (lax.div(i, across), lax.rem(i, across))
        self.c0.wait_recv()
        self.pair[...] = self.part[core] + self.rc[...]
        self.out.start(lambda to: self.pair.at[place(to)], lambda i: self.rz.at[i])
        yield
        self.out.wait()
        me = place(z.me)
        self.full[(core,) + me] = self.pair[me] + jnp.sum(self.rz[...], axis=0)
        own = self.full.at[(core,) + me]
        self.back.start(lambda to: own, lambda i: own)
        yield
        self.back.wait()
        half = self.full.at[core]
        c1 = self.copies.send(self.g.sibling, half, half)
        yield
        c1.wait_recv()


def kernel(nx, ny, nz, a_hbm, t_hbm, first_hbm, basis_hbm, proj_hbm, a_ref, t_ref, work, lhs_ref, terms_ref, turned_ref,
           inv0, inv1, first_ref, basis_ref, proj_ref, a_sem, t_sem, out_sem, *refs):
    g = Grid(nx, ny, nz)
    rows, dims = a_ref.shape
    h = dims // 2
    gr = RANK // (nx * ny)
    ranks = RANK // CHUNKS
    refs = list(refs)

    def take(kind, *sizes):
        n = len(kind.scratch(*sizes))
        out = kind(g, refs[:n])
        del refs[:n]
        return out

    feats, grams, exs = [], [], []
    for _ in range(2):
        feats.append([take(FeatSum, nx, ny, ranks, rows) for _ in range(CHUNKS)])
        grams.append(take(GramSum, nx, ny, nz))
        exs.append([take(ExSum, nz, ranks, dims) for _ in range(CHUNKS)])

    load_t = pltpu.make_async_copy(t_hbm, t_ref, t_sem)
    load_t.start()
    load_a = pltpu.make_async_copy(a_hbm, a_ref, a_sem)
    load_a.start()
    greeted = g.greet()

    scale = jnp.sqrt(jnp.float32(ROWS))
    shrink = 1.0 / jnp.sqrt(jnp.float32(DIMS))
    invs, outs = (inv0, inv1), ((first_ref, first_hbm), (basis_ref, basis_hbm))
    e = rows // (nx * ny)
    places = [(y, x) for y in range(ny) for x in range(nx)]

    def turn(s):
        for n, at in enumerate(places):
            block = jnp.concatenate([feats[s][c].full[at] for c in range(CHUNKS)], axis=0)
            turned_ref[n * e : (n + 1) * e, :] = block.T

    def write_rows(s):
        ref, hbm = outs[s]
        ref[...] = scale * lax.dot_general(
            turned_ref[...], invs[s][...], (((1,), (1,)), ((), ())), preferred_element_type=F32, precision=HIGHEST
        )
        copy = pltpu.make_async_copy(ref, hbm, out_sem.at[s])
        copy.start()
        return copy

    def own_gram(s):
        terms = terms_ref[...]
        raw = lax.dot_general(terms, terms, (((1,), (1,)), ((), ())), preferred_element_type=F32)
        for c in range(CHUNKS):
            r0 = 2 * c * ranks
            some = raw[r0 : r0 + ranks] + raw[r0 + ranks : r0 + 2 * ranks]
            parts = []
            for d in range(CHUNKS):
                c0 = 2 * d * ranks
                parts.append(some[:, c0 : c0 + ranks] + some[:, c0 + ranks : c0 + 2 * ranks])
            work[c * ranks : (c + 1) * ranks, 0:RANK] = jnp.concatenate(parts, axis=1)
        at = pl.ds(pl.multiple_of((g.y.me * nx + g.x.me) * gr, gr), gr)
        grams[s].own[...] = work[at, 0:RANK]

    def chain(s, c):
        feat, ex = feats[s][c], exs[s][c]
        prod = lax.dot_general(
            lhs_ref[c * ranks : (c + 1) * ranks, :], a_ref[...], (((1,), (1,)), ((), ())), preferred_element_type=F32
        )
        for n, at in enumerate(places):
            feat.part[at] = prod[:, n * e : (n + 1) * e]
        if s == 0 and c == 0:
            greeted()
        yield from feat.run()
        for n, at in enumerate(places):
            high, low = split(feat.full[at])
            terms_ref[2 * c * ranks : (2 * c + 1) * ranks, n * e : (n + 1) * e] = high
            terms_ref[(2 * c + 1) * ranks : (2 * c + 2) * ranks, n * e : (n + 1) * e] = low
        yield
        for n in range(2):
            side = 1 - g.core if n == 0 else g.core
            at = pl.ds(pl.multiple_of(side * h, h), h)
            prod = jnp.dot(terms_ref[2 * c * ranks : (2 * c + 2) * ranks, :], a_ref[:, at], preferred_element_type=F32)
            ex.put(side, prod[:ranks] + prod[ranks:])
            if n == 0:
                ex.start()
        yield
        yield from ex.run()

    def applied(s, c, side):
        out = 0.0
        for d in range(c + 1):
            inv = invs[s][c * ranks : (c + 1) * ranks, d * ranks : (d + 1) * ranks]
            out += jnp.dot(inv, exs[s][d].get(side), preferred_element_type=F32, precision=HIGHEST)
        return out

    load_t.wait()
    lhs_ref[...] = t_ref[...].astype(F32).T.astype(BF16)
    load_a.wait()
    chains = [chain(0, c) for c in range(CHUNKS)]
    for one in chains:
        next(one)
    for s in range(2):
        for _ in range(3):
            for one in chains:
                next(one)
        gram = grams[s].run()
        for c, one in enumerate(chains):
            next(one)
            if c == CHUNKS - 1:
                own_gram(s)
                next(gram)
            next(one)
            if c == CHUNKS - 1:
                next(gram)
            next(one)
        turn(s)
        next(chains[0])
        next(gram)
        for one in chains[1:]:
            next(one)
        next(gram)
        next(gram, None)
        work[:, 0:RANK] = grams[s].full[...].reshape(RANK, RANK)
        row = lax.broadcasted_iota(jnp.int32, (RANK, RANK), 0)
        column = lax.broadcasted_iota(jnp.int32, (RANK, RANK), 1)
        work[:, RANK : 2 * RANK] = jnp.where(row == column, 1.0, 0.0).astype(F32)
        panels = RANK // BLOCK
        factor(work, 0, panels // 2)
        if CHUNKS > 1:
            next(chains[0])
        factor(work, panels // 2, panels)
        invs[s][...] = work[:, RANK : 2 * RANK]
        if s == 1:
            out1 = write_rows(1)
        if CHUNKS == 1:
            next(chains[0])
        later = []
        for c in range(CHUNKS):
            if c > 0:
                next(chains[c])
            for n in range(2):
                side = g.core if n == 0 else 1 - g.core
                at = pl.ds(pl.multiple_of(side * h, h), h)
                if n == 1:
                    next(chains[c], None)
                if s == 0:
                    lhs_ref[c * ranks : (c + 1) * ranks, at] = (applied(s, c, side) * shrink).astype(BF16)
                else:
                    proj_ref[c * ranks : (c + 1) * ranks, at] = applied(s, c, side)
            if s == 0:
                later.append(chain(1, c))
                next(later[c])
        if s == 0:
            out0 = write_rows(0)
            chains = later
    out2 = pltpu.make_async_copy(proj_ref, proj_hbm, out_sem.at[2])
    out2.start()
    for s in range(2):
        for one in feats[s] + [grams[s]] + exs[s]:
            one.drain()
    out0.wait()
    out1.wait()
    out2.wait()


def shards(nx, ny, nz, features, test_matrix):
    rows, dims = features.shape
    ranks = RANK // CHUNKS
    hbm = pl.BlockSpec(memory_space=pl.ANY)
    scratch = [
        pltpu.VMEM((rows, dims), BF16),
        pltpu.VMEM((dims, RANK), BF16),
        pltpu.VMEM((RANK, 2 * RANK), F32),
        pltpu.VMEM((RANK, dims), BF16),
        pltpu.VMEM((2 * RANK, rows), BF16),
        pltpu.VMEM((rows, RANK), F32),
        pltpu.VMEM((RANK, RANK), F32),
        pltpu.VMEM((RANK, RANK), F32),
        pltpu.VMEM((rows, RANK), F32),
        pltpu.VMEM((rows, RANK), F32),
        pltpu.VMEM((RANK, dims), F32),
        pltpu.SemaphoreType.DMA,
        pltpu.SemaphoreType.DMA,
        pltpu.SemaphoreType.DMA((3,)),
    ]
    for _ in range(2):
        scratch += FeatSum.scratch(nx, ny, ranks, rows) * CHUNKS
        scratch += GramSum.scratch(nx, ny, nz)
        scratch += ExSum.scratch(nz, ranks, dims) * CHUNKS
    return pl.pallas_call(
        functools.partial(kernel, nx, ny, nz),
        out_shape=(
            jax.ShapeDtypeStruct((rows, RANK), F32),
            jax.ShapeDtypeStruct((rows, RANK), F32),
            jax.ShapeDtypeStruct((RANK, dims), F32),
        ),
        in_specs=[hbm, hbm],
        out_specs=(hbm, hbm, hbm),
        scratch_shapes=scratch,
        compiler_params=pltpu.CompilerParams(
            collective_id=0, has_side_effects=True, vmem_limit_bytes=48 * 1024 * 1024
        ),
        cost_estimate=pl.CostEstimate(flops=6 * rows * dims * RANK * 2, bytes_accessed=8 << 20, transcendentals=256),
    )(features, test_matrix)


def solution(mesh):
    feat, ex = mesh.shape["feat"], mesh.shape["ex"]
    nx = 4
    return jax.shard_map(
        functools.partial(shards, nx, feat // nx, ex // 2),
        mesh=mesh,
        in_specs=(P("ex", "feat"), P("feat", None)),
        out_specs=(P("ex", None), P("ex", None), P(None, "feat")),
        check_vma=False,
    )
```

time: 1100 us -> 134 us (0.12)
  waiting for transfers between devices: 1010 us -> 0 us
  Pallas kernels: 0 us -> 129 us
  other arithmetic: 47.6 us -> 0 us
  matrix products: 27.2 us -> 0 us
  between operations: 14.2 us -> 0.65 us
    psum x6 -> x0, waiting for transfers between devices: 1010 us -> none  [the longest x1 201 us: shards(): power_total = lax.psum(power_part, 'ex')]
    pallas_call x0 -> x1, Pallas kernels: none -> 129 us  [shards(): pl.pallas_call(functools.partial(kernel, nx, ny, nz), out_shape=(jax.Shap...]
    another operation x10 -> x0, other arithmetic: 45.7 us -> none  [the longest x6 24.8 us: solve_rows(): lower = jnp.linalg.cholesky(gram)]
    dot_general x6 -> x0, matrix products: 23.9 us -> none  [the longest x2 7.25 us: own_gram(): jnp.dot(sketch.T, sketch, preferred_element_type=jnp.float32, precision=l...]
  transfers between devices with their start and end apart: 6 -> 0, of which waited for: 6 -> 0; matrix products, arithmetic and copies ran while one was open for 0% -> 0% of each run, Pallas kernels for 0% -> 0%
where the time goes in v2:
time: 134 us; the launch traced here: 133 us
  Pallas kernels  129 us (96%)
  local copies, waits for them, and re-layouts  3.68 us (3%)
    pallas_call x1, Pallas kernels, shards(): pl.pallas_call(functools.partial(kernel, nx, ny, nz), out_shape=(jax.Shap...  129 us
    unnamed x5, local copies, waits for them, and re-layouts  3.68 us

profile of v2, /device:TPU:1, one launch (start us, length us, event | category | flops | bytes accessed | tf_op | source)
XLA Modules:
  0.0 133.4 jit_solution(15406883518584193283)
XLA Ops:
  0.6 0.0 copy-start
  0.6 0.9 copy-done
  1.6 129.1 %shard_map.49 = (f32[2048,128]{1,0:T(8,128)S(1)}, f32[2048,128]{1,0:T(8,128)S(1)}, f32[128,1024]{1,0:T(8,128)S(1)}) custom-call(bf16[2048,1024]{1,0:T(8,128)(2,1)} %a_hbm.1, bf16[1024,128]{1,0:T(8,128)(2,1)S(1)} %copy-done), custom_call_target="tpu_custom_call" | custom-call | flops 3221225472 | bytes 8388608 | tf_op jit(solution)/shard_map/pallas_call | solution.py:518
  130.7 1.0 copy.8
  131.6 1.0 copy.9
  132.6 0.8 copy.10
Async XLA Ops:
  0.6 1.0 copy-start

commit v3 on v2

--- a/solution.py
+++ b/solution.py
@@ -15,6 +15,7 @@
 BF16 = jnp.bfloat16
 HIGHEST = lax.Precision.HIGHEST
 BLOCK = 8
+EARLY = 4
 CHUNKS = 2
 
 
@@ -225,14 +226,14 @@
 class GramSum:
     @staticmethod
     def scratch(nx, ny, nz):
-        r = RANK // (nx * ny)
+        r = RANK // (nx * ny) // 2
         return [
-            pltpu.VMEM((r, RANK), F32),
+            pltpu.VMEM((2, r, RANK), F32),
             pltpu.VMEM((r, RANK), F32),
             pltpu.VMEM((r, RANK), F32),
             pltpu.VMEM((nz - 1, r, RANK), F32),
-            pltpu.VMEM((ny, nx, r, RANK), F32),
-        ] + Copies.scratch(1) + Along.scratch(nz) + Along.scratch(nx) + Along.scratch(ny)
+            pltpu.VMEM((ny, nx, 2, r, RANK), F32),
+        ] + Copies.scratch(2) + Along.scratch(nz) + Along.scratch(nx) + Along.scratch(ny)
 
     def __init__(self, grid, refs):
         self.g = grid
@@ -247,14 +248,17 @@
 
     def run(self):
         g = self.g
-        across = self.copies.send(g.sibling, self.own, self.rc)
+        across = self.copies.send(g.sibling, self.own.at[1 - g.core], self.rc)
         yield
         across.wait_recv()
-        self.pair[...] = self.own[...] + self.rc[...]
+        self.pair[...] = self.own[g.core] + self.rc[...]
         self.az.start(lambda to: self.pair, lambda i: self.rz.at[i])
         yield
         self.az.wait()
-        self.full[g.y.me, g.x.me] = self.pair[...] + jnp.sum(self.rz[...], axis=0)
+        mine = self.full.at[g.y.me, g.x.me, g.core]
+        mine[...] = self.pair[...] + jnp.sum(self.rz[...], axis=0)
+        across = self.copies.send(g.sibling, mine, mine)
+        across.wait_recv()
         own, row = self.full.at[g.y.me, g.x.me], self.full.at[g.y.me]
         self.ax.start(lambda to: own, lambda i: own)
         yield
@@ -387,7 +391,9 @@
                 parts.append(some[:, c0 : c0 + ranks] + some[:, c0 + ranks : c0 + 2 * ranks])
             work[c * ranks : (c + 1) * ranks, 0:RANK] = jnp.concatenate(parts, axis=1)
         at = pl.ds(pl.multiple_of((g.y.me * nx + g.x.me) * gr, gr), gr)
-        grams[s].own[...] = work[at, 0:RANK]
+        own = work[at, 0:RANK]
+        for n in range(2):
+            grams[s].own[n] = own[n * (gr // 2) : (n + 1) * (gr // 2)]
 
     def chain(s, c):
         feat, ex = feats[s][c], exs[s][c]
@@ -411,7 +417,7 @@
             ex.put(side, prod[:ranks] + prod[ranks:])
             if n == 0:
                 ex.start()
-        yield
+            yield
         yield from ex.run()
 
     def applied(s, c, side):
@@ -432,40 +438,39 @@
             for one in chains:
                 next(one)
         gram = grams[s].run()
+        for one in chains:
+            next(one)
+        own_gram(s)
+        next(gram)
         for c, one in enumerate(chains):
             next(one)
-            if c == CHUNKS - 1:
-                own_gram(s)
+            if c == 0:
                 next(gram)
             next(one)
-            if c == CHUNKS - 1:
-                next(gram)
-            next(one)
-        turn(s)
-        next(chains[0])
-        next(gram)
-        for one in chains[1:]:
             next(one)
         next(gram)
+        turn(s)
+        next(gram)
+        next(chains[0])
         next(gram, None)
-        work[:, 0:RANK] = grams[s].full[...].reshape(RANK, RANK)
+        for n, (y, x) in enumerate(places):
+            for half in range(2):
+                begin = n * gr + half * (gr // 2)
+                work[begin : begin + gr // 2, 0:RANK] = grams[s].full[y, x, half]
         row = lax.broadcasted_iota(jnp.int32, (RANK, RANK), 0)
         column = lax.broadcasted_iota(jnp.int32, (RANK, RANK), 1)
         work[:, RANK : 2 * RANK] = jnp.where(row == column, 1.0, 0.0).astype(F32)
         panels = RANK // BLOCK
-        factor(work, 0, panels // 2)
-        if CHUNKS > 1:
-            next(chains[0])
-        factor(work, panels // 2, panels)
+        factor(work, 0, EARLY)
+        for one in chains[1:]:
+            next(one)
+        factor(work, EARLY, panels)
         invs[s][...] = work[:, RANK : 2 * RANK]
         if s == 1:
             out1 = write_rows(1)
-        if CHUNKS == 1:
-            next(chains[0])
         later = []
         for c in range(CHUNKS):
-            if c > 0:
-                next(chains[c])
+            next(chains[c])
             for n in range(2):
                 side = g.core if n == 0 else 1 - g.core
                 at = pl.ds(pl.multiple_of(side * h, h), h)

time: 134 us -> 130 us (0.970)
  Pallas kernels: 129 us -> 125 us
    pallas_call x1, Pallas kernels: 129 us -> 125 us  [shards(): pl.pallas_call(functools.partial(kernel, nx, ny, nz), out_shape=(jax.Shap...]
where the time goes in v3:
time: 130 us
  Pallas kernels  125 us (96%)
  local copies, waits for them, and re-layouts  3.68 us (3%)
    pallas_call x1, Pallas kernels, shards(): pl.pallas_call(functools.partial(kernel, nx, ny, nz), out_shape=(jax.Shap...  125 us
    unnamed x5, local copies, waits for them, and re-layouts  3.68 us

profile of v3, /device:TPU:1, one launch (start us, length us, event | category | flops | bytes accessed | tf_op | source)
XLA Modules:
  0.0 129.6 jit_solution(5870210919272316902)
XLA Ops:
  0.6 0.0 copy-start
  0.6 0.9 copy-done
  1.6 125.3 %shard_map.49 = (f32[2048,128]{1,0:T(8,128)S(1)}, f32[2048,128]{1,0:T(8,128)S(1)}, f32[128,1024]{1,0:T(8,128)S(1)}) custom-call(bf16[2048,1024]{1,0:T(8,128)(2,1)} %a_hbm.1, bf16[1024,128]{1,0:T(8,128)(2,1)S(1)} %copy-done), custom_call_target="tpu_custom_call" | custom-call | flops 3221225472 | bytes 8388608 | tf_op jit(solution)/shard_map/pallas_call | solution.py:523
  126.9 1.0 copy.8
  127.8 1.0 copy.9
  128.8 0.8 copy.10
Async XLA Ops:
  0.6 1.0 copy-start
